TPU v7x, 32 devices: a whole 2x2x4 slice. The times are simulated.
32 devices in a mesh: row: 4 (over x, core), col: 8 (over z, y).
Axes of the slice: x: 2, y: 2, z: 4, core: 2. Of those that a mesh axis runs over, the one named last changes fastest.
Arguments:
- amplitudes: float32 [4096, 2048], P('row', 'col'), may hold values from -6 to 6
- pp_integrals: float32 [2048, 2048], P('row', 'col'), may hold values from -2.5 to 2.5
- hole_fock: float32 [64, 64], replicated, may hold values from -0.75 to 0.75
- tile_pattern: int32 [64, 32], P('row', 'col'), may hold values 0 or 1
- integral_pattern: int32 [32, 32], P('row', 'col'), may hold values 0 or 1
- tile_extent: int32 [32], P('col'), may hold values from 40 to 64
- tile_owner: int32 [8, 4], P('col'), may hold values from 0 to 3, each once within a row
Outputs:
- residual_owned: float32 [32, 64, 4096], P(('row', 'col'))
Inputs may be any that keep to these rules, and one draw needn't show every extreme that they name: Each row of tile_owner names every tile of its group once.
All inputs are finite; a program needn't handle non-finite values. No bound on the sum of `tile_pattern` or of `integral_pattern` on one device may be relied on, other than what follows from the above.
Results may differ from a plain program's by a relative error of at most 0.000067.
Values sent between devices are 32-bit elements; how exact they have to be, the bound alone decides.
No kernel may reach another device: no remote copies, remote signals or barrier semaphores. Data moves between devices by JAX's collectives and lax.ppermute only.
A program may use at most 128 MiB of HBM per device.

v0:
```python
import jax
import jax.numpy as jnp
from jax import lax
from jax.experimental import pallas as pl
from jax.experimental.pallas import tpu as pltpu
from jax.sharding import PartitionSpec as P

NO = 64
TS = 64
HALF = TS // 2
LANES = 2 * TS
ROW_SLOTS = 16
COL_SLOTS = (2, 4)
HIGHEST = lax.Precision.HIGHEST


def gather_exchange(values, axis):
    count = lax.axis_size(axis)
    copies = jnp.broadcast_to(values[None], (count,) + values.shape)
    return lax.all_to_all(copies, axis, split_axis=0, concat_axis=0)


def occupied_term(moved, hole_fock):
    shape_in = moved.shape
    paired = moved.reshape(NO, NO, shape_in[1] * shape_in[2])
    result = jnp.einsum("ik,kjc->ijc", hole_fock, paired, precision=HIGHEST)
    result = result + jnp.einsum("jk,ikc->ijc", hole_fock, paired, precision=HIGHEST)
    return result.reshape(shape_in)


def dense(
    amplitudes, pp_integrals, hole_fock, tile_pattern, integral_pattern, tile_extent, tile_owner
):
    row_count, col_count = amplitudes.shape
    groups = tile_extent.shape[0]
    col_keep = (lax.broadcasted_iota(jnp.int32, (groups, TS), 1) < tile_extent[:, None]).astype(
        jnp.float32
    )
    pattern_float = tile_pattern.astype(jnp.float32)
    keep_mask = (
        jnp.repeat(jnp.repeat(pattern_float, TS, 0), TS, 1) * col_keep.reshape(col_count)[None, :]
    )
    masked = amplitudes * keep_mask
    integrals = pp_integrals * jnp.repeat(
        jnp.repeat(integral_pattern.astype(jnp.float32), TS, 0), TS, 1
    )
    owner_list = tile_owner[0]
    slot_count = groups // lax.axis_size("row")
    my_tiles = lax.dynamic_slice_in_dim(owner_list, lax.axis_index("row") * slot_count, slot_count)

    def ordered(values):
        return jnp.take(values.reshape(values.shape[0], groups, TS), owner_list, axis=1)

    pattern_sent = jnp.take(pattern_float, owner_list, axis=1)
    column_block = gather_exchange(integrals, "row")
    column_block = column_block.reshape(-1, col_count)
    row_block = gather_exchange(masked, "col")
    row_block = jnp.transpose(row_block, (1, 0, 2)).reshape(row_count, -1)
    ladder = jnp.dot(
        row_block, column_block, precision=HIGHEST, preferred_element_type=jnp.float32
    )
    moved_amps, moved_ladder, moved_pattern = (
        lax.all_to_all(ordered(masked), "row", split_axis=1, concat_axis=0, tiled=True),
        lax.all_to_all(ordered(ladder), "row", split_axis=1, concat_axis=0, tiled=True),
        lax.all_to_all(pattern_sent, "row", split_axis=1, concat_axis=0, tiled=True),
    )
    occupied = occupied_term(moved_amps, hole_fock)
    extents = jnp.take(tile_extent, my_tiles)
    extent_keep = (lax.broadcasted_iota(jnp.int32, (slot_count, TS), 1) < extents[:, None]).astype(
        jnp.float32
    )
    final_keep = jnp.repeat(moved_pattern, TS, 0)[:, :, None] * extent_keep[None, :, :]
    full = (moved_ladder + occupied) * final_keep
    return jnp.transpose(full, (1, 2, 0))


class Layout:
    def __init__(self, rows, cols, row_tiles, integral_tiles, groups):
        self.rows, self.cols, self.groups = rows, cols, groups
        self.row_tiles, self.integral_tiles = row_tiles, integral_tiles
        self.integral_at = groups * row_tiles
        self.owner_at = self.integral_at + groups * integral_tiles
        self.count_at = self.owner_at + groups
        self.width = -(-(self.count_at + 1) // 128) * 128

    def amp(self, info, row, tile, col, local):
        return info[row * self.cols + col, 0, local * self.row_tiles + tile]

    def integral(self, info, row, tile, col, local):
        return info[row * self.cols + col, 0, self.integral_at + local * self.integral_tiles + tile]

    def owner(self, info, row, col):
        return info[col, 0, self.owner_at + row]


def present(code):
    return jnp.minimum(code, 1)


def slot_rows(slot):
    return pl.ds(pl.multiple_of(slot * HALF, HALF), HALF)


def load_transposed(source, turn, tile, local, extent):
    lanes = pl.multiple_of((local >> 1) * LANES, LANES)
    rows = pl.multiple_of(tile * TS, TS)
    turn[...] = source[pl.ds(rows, TS), pl.ds(lanes, LANES)].T
    start = pl.multiple_of((local & 1) * TS, TS)
    upper = turn[pl.ds(start, HALF), :]
    lower = turn[pl.ds(start + HALF, HALF), :]
    if extent is not None:
        position = lax.broadcasted_iota(jnp.int32, (HALF, TS), 0)
        upper = jnp.where(position < extent, upper, 0.0)
        lower = jnp.where(position + HALF < extent, lower, 0.0)
    return jnp.concatenate([upper, lower], axis=1)


def unfold(packed):
    return jnp.concatenate([packed[:, :TS], packed[:, TS:]], axis=0)


def fold(tile):
    return jnp.concatenate([tile[:HALF], tile[HALF:]], axis=1)


def iota(shape, axis):
    return lax.broadcasted_iota(jnp.int32, shape, axis)


def pack_kernel(
    lay, amp_bits, int_bits, extent, amp_vec, int_vec, owner_vec, amps, ints, packed, info_out, turn, items
):
    pieces = [amp_vec[q : q + 1, :] for q in range(lay.groups)]
    pieces += [int_vec[q : q + 1, :] for q in range(lay.groups)]
    pieces += [owner_vec[...], jnp.zeros((1, lay.width - lay.count_at), jnp.int32)]
    entries = jnp.concatenate(pieces, axis=1).astype(jnp.float32)
    lane = iota((1, lay.width), 1)
    bits = jnp.where(lane < lay.owner_at, entries, 0.0)
    ahead = (iota((lay.width, lay.width), 0) <= iota((lay.width, lay.width), 1)).astype(jnp.float32)
    ranks = jnp.dot(
        jnp.broadcast_to(bits, (8, lay.width)), ahead, preferred_element_type=jnp.float32
    )[:1]
    row = jnp.where(lane < lay.owner_at, bits * ranks, entries)
    row = jnp.where(lane == lay.count_at, ranks, row).astype(jnp.int32)
    info_out[...] = jnp.broadcast_to(row[None], info_out.shape)
    n_amp = jnp.int32(0)
    for local in range(lay.groups):
        for tile in range(lay.row_tiles):
            items[n_amp] = tile * 256 + local
            n_amp += amp_bits[local, tile]
    n_all = n_amp
    for local in range(lay.groups):
        for tile in range(lay.integral_tiles):
            items[n_all] = tile * 256 + local
            n_all += int_bits[local, tile]

    def place(source, with_extent):
        def body(slot, carry):
            item = items[slot]
            local, tile = item & 255, item >> 8
            packed[slot_rows(slot), :] = load_transposed(
                source, turn, tile, local, extent[local] if with_extent else None
            )
            return carry

        return body

    n_amp = jnp.minimum(n_amp, ROW_SLOTS)
    n_all = jnp.minimum(n_all, ROW_SLOTS)
    lax.fori_loop(0, n_amp, place(amps, True), 0)
    lax.fori_loop(n_amp, n_all, place(ints, False), 0)


def check_kernel(lay, info, result):
    codes = info[:, 0, :]
    here = jnp.minimum(codes, 1).astype(jnp.float32)
    lane = iota((1, lay.width), 1)
    contract = (((1,), (1,)), ((), ()))

    def field(start, length, block):
        shift = (lay.width - start) % lay.width
        moved = pltpu.roll(here, shift, 1) if shift else here
        return jnp.where(lane < length, moved, 0.0).reshape(lay.rows, lay.cols, lay.width)[block]

    shared = None
    for row in range(lay.rows):
        stack = jnp.concatenate(
            [field(q * lay.row_tiles, lay.row_tiles, row) for q in range(lay.groups)], axis=0
        )
        term = lax.dot_general(stack, stack, contract, preferred_element_type=jnp.float32)
        shared = term if shared is None else shared + term
    total = lay.groups * lay.cols
    tiles = lay.rows * lay.integral_tiles
    at, to = iota((total, tiles), 0), iota((total, tiles), 1)
    order = (at == (to % lay.groups) * lay.cols + to // lay.groups).astype(jnp.float32)
    shared = jnp.dot(shared, order, preferred_element_type=jnp.float32)
    at, to = iota((total, tiles), 0), iota((total, tiles), 1)
    own = to == (at % lay.cols) * lay.groups + at // lay.cols
    shared = jnp.where(own, 0.0, shared)
    counts = None
    for row in range(lay.rows):
        stack = jnp.concatenate(
            [
                field(lay.integral_at + q * lay.integral_tiles, lay.integral_tiles, row)
                for q in range(lay.groups)
            ],
            axis=0,
        )
        wide = stack[:, : lay.integral_tiles]
        mine = wide * shared[:, row * lay.integral_tiles : (row + 1) * lay.integral_tiles]
        at, to = iota((lay.integral_tiles, 128), 0), iota((lay.integral_tiles, 128), 1)
        group = (at // lay.groups == to).astype(jnp.float32)
        term = jnp.dot(mine, group, preferred_element_type=jnp.float32)
        counts = term if counts is None else jnp.maximum(counts, term)
    most = jnp.max(counts)
    used = jnp.max(jnp.where(lane == lay.count_at, codes, 0))
    level = jnp.where(most > COL_SLOTS[0], 1, 0)
    result[0] = jnp.where((most > COL_SLOTS[1]) | (used > ROW_SLOTS), 2, level)


def forward_kernel(lay, slots, info, *refs):
    packed, (out, pairs, lists) = refs[: lay.rows], refs[lay.rows :]
    row, col = lax.axis_index("row"), lax.axis_index("col")
    base = col * lay.groups
    int_row, int_tile = base // lay.integral_tiles, base % lay.integral_tiles
    n_pairs = jnp.int32(0)
    for target in range(lay.cols):
        wanted = lay.owner(info, row, target)
        for local in range(lay.groups):
            pairs[n_pairs] = target * 256 + local
            hit = present(lay.integral(info, int_row, int_tile + local, target, wanted))
            n_pairs += jnp.where((target == col) & (wanted == local), 0, hit)

    def scan(index, carry):
        counts, previous, slot = carry
        pair = pairs[index]
        local, target = pair & 255, pair >> 8
        wanted = lay.owner(info, row, target)
        slot = jnp.where(target == previous, slot, 0)
        updated = []
        for k in range(lay.rows):
            count = counts[k]
            for tile in range(lay.row_tiles):
                code = lay.amp(info, row ^ k, tile, col, local)
                hit = present(code * lay.amp(info, row ^ k, tile, target, wanted))
                lists[k, count] = ((target * 256) + jnp.minimum(slot, 255)) * 256 + code - 1
                count += hit
                slot += hit
            updated.append(jnp.minimum(count, lay.cols * slots))
        return tuple(updated), target, slot

    zero = jnp.int32(0)
    counts, _, _ = lax.fori_loop(0, n_pairs, scan, ((zero,) * lay.rows, jnp.int32(-1), zero))
    for k in range(lay.rows):

        def send(index, carry, k=k):
            item = lists[k, index]
            source, slot, target = item & 255, (item >> 8) & 255, item >> 16

            @pl.when((slot < slots) & (source < ROW_SLOTS))
            def _():
                out[target, slot_rows(slot), :] = packed[k][slot_rows(source), :]

            return carry

        lax.fori_loop(0, counts[k], send, 0)


def finish_kernel(lay, info, extent, fock_scalar, fock, received, *refs):
    packed = refs[: lay.rows]
    out, amp_id, int_id, next_slot, tiles, ints, sums = refs[lay.rows :]
    row, col = lax.axis_index("row"), lax.axis_index("col")
    local = lay.owner(info, row, col)
    limit = extent[local]
    out[...] = jnp.zeros_like(out)
    for source in range(lay.cols):
        next_slot[source] = 0
    n_amp = jnp.int32(0)
    n_int = jnp.int32(0)
    for k in range(lay.rows):
        first = n_amp
        for tile in range(lay.row_tiles):
            code = lay.amp(info, row ^ k, tile, col, local)
            amp_id[n_amp] = ((row ^ k) * lay.row_tiles + tile) * 256 + code - 1
            n_amp += present(code)

        def take_amp(index, carry, k=k):
            tiles[slot_rows(index), :] = packed[k][slot_rows(amp_id[index] & 255), :]
            return carry

        lax.fori_loop(first, n_amp, take_amp, 0)
        first = n_int
        for tile in range(lay.integral_tiles):
            code = lay.integral(info, row ^ k, tile, col, local)
            int_id[n_int] = ((row ^ k) * lay.integral_tiles + tile) * 256 + code - 1
            n_int += present(code)

        def take_int(index, carry, k=k):
            ints[slot_rows(index), :] = packed[k][slot_rows(int_id[index] & 255), :]
            return carry

        lax.fori_loop(first, n_int, take_int, 0)

    blank = jnp.zeros((TS, TS), jnp.float32)
    both = jnp.concatenate(
        [
            jnp.concatenate([fock[...], blank], axis=1),
            jnp.concatenate([blank, fock[...]], axis=1),
        ],
        axis=0,
    )
    chunk = 4 * HALF

    def second(index, carry):
        rows = pl.ds(pl.multiple_of(index * chunk, chunk), chunk)
        sums[rows, :] = lax.dot_general(
            tiles[rows, :],
            both,
            (((1,), (1,)), ((), ())),
            precision=HIGHEST,
            preferred_element_type=jnp.float32,
        )
        return carry

    lax.fori_loop(0, (n_amp + 3) >> 2, second, 0)

    def ladder(which, carry):
        middle = int_id[which] >> 8
        source, middle_local = middle // lay.groups, middle % lay.groups
        own = (source == col) & (middle_local == local)

        def add(index, packed_tile):
            product = jnp.dot(
                unfold(ints[slot_rows(which), :]),
                unfold(packed_tile),
                precision=HIGHEST,
                preferred_element_type=jnp.float32,
            )
            product = jnp.where(iota((TS, TS), 0) < limit, product, 0.0)
            sums[slot_rows(index), :] += fold(product)

        def per_tile(index, carry):
            tile = amp_id[index] >> 8
            code = lay.amp(info, tile // lay.row_tiles, tile % lay.row_tiles, source, middle_local)

            @pl.when(own)
            def _():
                add(index, tiles[slot_rows(index), :])

            @pl.when((code > 0) & ~own)
            def _():
                slot = next_slot[source]
                next_slot[source] = slot + 1
                add(index, received[source, slot_rows(slot), :])

            return carry

        return lax.fori_loop(0, n_amp, per_tile, carry)

    lax.fori_loop(0, n_int, ladder, 0)

    def write(index, carry):
        tile = amp_id[index] >> 8

        def first(other, value):
            return value + fock_scalar[tile, amp_id[other] >> 8] * tiles[slot_rows(other), :]

        value = lax.fori_loop(0, n_amp, first, sums[slot_rows(index), :])
        turned = pltpu.roll(value, TS, 1)
        odd = tile & 1
        lanes = pl.ds(pl.multiple_of((tile >> 1) * LANES, LANES), LANES)
        side = iota((HALF, LANES), 1) // TS == odd
        is_odd = iota((HALF, LANES), 0) * 0 + odd == 1
        upper = jnp.where(is_odd, turned, value)
        lower = jnp.where(is_odd, value, turned)
        out[0, :HALF, lanes] = jnp.where(side, upper, out[0, :HALF, lanes])
        out[0, HALF:, lanes] = jnp.where(side, lower, out[0, HALF:, lanes])
        return carry

    lax.fori_loop(0, n_amp, write, 0)


def local(
    amplitudes, pp_integrals, hole_fock, tile_pattern, integral_pattern, tile_extent, tile_owner
):
    rows, cols = lax.axis_size("row"), lax.axis_size("col")
    groups = tile_extent.shape[0]
    arguments = (
        amplitudes,
        pp_integrals,
        hole_fock,
        tile_pattern,
        integral_pattern,
        tile_extent,
        tile_owner,
    )
    row_tiles, integral_tiles = tile_pattern.shape[0], integral_pattern.shape[0]
    if groups != rows or integral_tiles % groups or rows & (rows - 1):
        return dense(*arguments)
    lay = Layout(rows, cols, row_tiles, integral_tiles, groups)
    devices = rows * cols

    def smem(shape):
        return pltpu.SMEM(shape, jnp.int32)

    in_smem = pl.BlockSpec(memory_space=pltpu.SMEM)
    in_vmem = pl.BlockSpec(memory_space=pltpu.VMEM)
    params = pltpu.CompilerParams(vmem_limit_bytes=32 * 2**20)
    packed_shape = (ROW_SLOTS * HALF, LANES)

    packed, mine = pl.pallas_call(
        lambda *refs: pack_kernel(lay, *refs),
        out_shape=(
            jax.ShapeDtypeStruct(packed_shape, jnp.float32),
            jax.ShapeDtypeStruct((devices, 1, lay.width), jnp.int32),
        ),
        in_specs=[in_smem] * 3 + [in_vmem] * 5,
        out_specs=(in_vmem, in_vmem),
        scratch_shapes=[
            pltpu.VMEM((LANES, TS), jnp.float32),
            smem(((row_tiles + integral_tiles) * groups + 1,)),
        ],
        compiler_params=params,
        name="pack_tiles",
    )(
        tile_pattern.T,
        integral_pattern.T,
        tile_extent,
        tile_pattern.T,
        integral_pattern.T,
        tile_owner,
        amplitudes,
        pp_integrals,
    )
    shares = [packed]
    for k in range(1, rows):
        shares.append(lax.ppermute(packed, "row", [(i, i ^ k) for i in range(rows)]))
    info = lax.all_to_all(mine, ("row", "col"), split_axis=0, concat_axis=0, tiled=True)

    level = pl.pallas_call(
        lambda *refs: check_kernel(lay, *refs),
        out_shape=jax.ShapeDtypeStruct((1,), jnp.int32),
        in_specs=[in_vmem],
        out_specs=in_smem,
        compiler_params=params,
        name="check_slots",
    )(info)

    def forward(slots, info, *shares):
        col_send = pl.pallas_call(
            lambda *refs: forward_kernel(lay, slots, *refs),
            out_shape=jax.ShapeDtypeStruct((cols, slots * HALF, LANES), jnp.float32),
            in_specs=[in_smem] + [in_vmem] * rows,
            out_specs=in_vmem,
            scratch_shapes=[
                smem((cols * groups + 1,)),
                smem((rows, cols * slots + row_tiles + 1)),
            ],
            compiler_params=params,
            name="forward_tiles",
        )(info, *shares)
        return lax.all_to_all(col_send, "col", split_axis=0, concat_axis=0, tiled=True)

    received = forward(COL_SLOTS[0], info, *shares)

    def finish(info, received, shares, arguments):
        return pl.pallas_call(
            lambda *refs: finish_kernel(lay, *refs),
            out_shape=jax.ShapeDtypeStruct((1, TS, rows * row_tiles * TS), jnp.float32),
            in_specs=[in_smem] * 3 + [in_vmem] * (2 + rows),
            out_specs=in_vmem,
            scratch_shapes=[
                smem((rows * row_tiles + 1,)),
                smem((rows * integral_tiles + 1,)),
                smem((cols,)),
                pltpu.VMEM((rows * (row_tiles + 1) * HALF, LANES), jnp.float32),
                pltpu.VMEM((rows * integral_tiles * HALF, LANES), jnp.float32),
                pltpu.VMEM((rows * (row_tiles + 1) * HALF, LANES), jnp.float32),
            ],
            compiler_params=params,
            name="finish_residual",
        )(info, arguments[5], arguments[2], arguments[2], received, *shares)

    def more_slots(info, received, shares, arguments):
        return finish(info, forward(COL_SLOTS[1], info, *shares), shares, arguments)

    def all_tiles(info, received, shares, arguments):
        return dense(*arguments)

    return lax.switch(
        level[0], (finish, more_slots, all_tiles), info, received, tuple(shares), arguments
    )


def solution(mesh):
    placed = (
        P("row", "col"),
        P("row", "col"),
        P(),
        P("row", "col"),
        P("row", "col"),
        P("col"),
        P("col", None),
    )
    return jax.shard_map(
        local, mesh=mesh, in_specs=placed, out_specs=P(("row", "col"), None, None), check_vma=False
    )
```

profile of v0, /device:TPU:0, one launch (start us, length us, event | category | flops | bytes accessed | tf_op | source)
XLA Modules:
  0.0 41.4 jit_solution(1161324490191402483)
XLA Ops:
  0.0 0.0 copy-start.4
  0.0 0.0 copy-start.7
  0.0 0.0 copy-start.3
  0.0 2.4 %pack_tiles.1 = (f32[512,128]{1,0:T(8,128)S(1)}, s32[32,1,128]{2,1,0:T(1,128)S(1)}) custom-call(s32[4,16]{1,0:T(4,128)} %bitcast.73, s32[4,8]{1,0:T(4,128)} %bitcast.75, s32[4]{0:T(128)} %refs_2_.1, s32[4,16]{1,0:T(4,128)} %bitcast.74, s32[4,8]{1,0:T(4,128)} %bitcast.76, s32[1,4]{1,0:T(1,128)} %refs_5_.1, f32[1024,256]{1,0:T(8,128)} %refs_6_.1, ...), custom_call_target="tpu_custom_call" | custom-call | tf_op jit(solution)/shard_map/pack_tiles/pallas_call | solution.py:411
  2.5 0.2 collective-permute-start
  2.6 2.9 %collective-permute-start.1 = (f32[512,128]{1,0:T(8,128)S(1)}, f32[512,128]{1,0:T(8,128)S(1)}, u32[]{:S(2)}, u32[]{:S(2)}) collective-permute-start(f32[512,128]{1,0:T(8,128)S(1)} %get-tuple-element.79.refs_1_), channel_id=1, source_target_pairs={{0,16},{8,24},{16,0},{24,8},{1,17},{9,25},{17,1},{25,9},{2,18},{10... | collective-permute-start | bytes 786440 | tf_op jit(solution)/shard_map/ppermute | solution.py:437
  5.5 0.1 collective-permute-start.2
  5.6 14.4 %all_to_all.62.refs_0_ = s32[32,1,128]{2,1,0:T(1,128)S(1)} all-to-all(s32[32,1,128]{2,1,0:T(1,128)S(1)} %get-tuple-element.78), channel_id=1, replica_groups=mesh['row'=4,'col'=8] {'row','col'}, dimensions={0} | all-to-all | bytes 32768 | tf_op jit(solution)/shard_map/all_to_all | solution.py:438
  20.0 0.0 collective-permute-done.refs_2_
  20.0 0.0 collective-permute-done.1.refs_3_
  20.0 0.0 collective-permute-done.2.refs_4_
  20.0 2.8 %forward_tiles.3 = f32[8,64,128]{2,1,0:T(8,128)} custom-call(s32[32,1,128]{2,1,0:T(1,128)S(1)} %all_to_all.62.refs_0_, f32[512,128]{1,0:T(8,128)S(1)} %get-tuple-element.79.refs_1_, f32[512,128]{1,0:T(8,128)S(1)} %collective-permute-done.refs_2_, f32[512,128]{1,0:T(8,128)S(1)} %collective-permute-done.1.refs_3_, f32[512,128]{1,0:T(8,128)S(1)} %collective-permute-done.2.refs_4_), custom_call_target="tpu_custom_call" | custom-call | tf_op jit(solution)/shard_map/forward_tiles/pallas_call | solution.py:450
  22.8 6.6 %all-to-all-start.7 = ((f32[8,64,128]{2,1,0:T(8,128)}), f32[8,64,128]{2,1,0:T(8,128)S(1)}, u32[]{:S(2)}, u32[]{:S(2)}) async-start(f32[8,64,128]{2,1,0:T(8,128)} %forward_tiles.3), calls=%async_computation.7 | async-start | bytes 524288 | tf_op jit(solution)/shard_map/all_to_all | solution.py:462
  29.4 1.2 %check_slots.1 = s32[1]{0:T(128)} custom-call(s32[32,1,128]{2,1,0:T(1,128)S(1)} %all_to_all.62.refs_0_), custom_call_target="tpu_custom_call" | custom-call | tf_op jit(solution)/shard_map/check_slots/pallas_call | solution.py:440
  31.2 6.4 %all-to-all-done.7 = f32[8,64,128]{2,1,0:T(8,128)S(1)} async-done(((f32[8,64,128]{2,1,0:T(8,128)}), f32[8,64,128]{2,1,0:T(8,128)S(1)}, u32[]{:S(2)}, u32[]{:S(2)}) %all-to-all-start.7) | async-done | bytes 262176 | tf_op jit(solution)/shard_map/all_to_all | solution.py:462
  37.6 0.0 copy-done.4
  37.7 0.0 copy-done.5
  37.7 0.0 copy-done.1
  37.7 0.0 copy-done.2
  37.7 0.0 copy-done.6
  37.7 0.0 copy-done.7
  37.7 0.0 copy-done.3
  37.7 3.7 %conditional.1 = (f32[1,64,4096]{2,1,0:T(8,128)}) conditional(s32[]{:T(128)} %bitcast.29, (s32[32,1,128]{2,1,0:T(1,128)S(1)}, s32[4]{0:T(128)S(1)}, f32[64,64]{1,0:T(8,128)S(1)}, f32[8,64,128]{2,1,0:T(8,128)S(1)}, f32[512,128]{1,0:T(8,128)S(1)}, /*index=5*/f32[512,128]{1,0:T(8,128)S(1)}, f32[512,128]{1,0:T(8,128)S(1)}, ...), branch_computations={%region_0.0_spmd, %region_1.0_spmd, %region_2.4_spmd} | conditional | flops 6847334912 | bytes 147542720 | solution.py:490
  37.7 3.7 %finish_residual.2 = f32[1,64,4096]{2,1,0:T(8,128)} custom-call(s32[32,1,128]{2,1,0:T(1,128)S(1)} %get-tuple-element.52.refs_0_, s32[4]{0:T(128)S(1)} %get-tuple-element.54.refs_1_, f32[64,64]{1,0:T(8,128)S(1)} %get-tuple-element.56.refs_2_.refs_3_, f32[64,64]{1,0:T(8,128)S(1)} %get-tuple-element.56.refs_2_.refs_3_, ...), custom_call_target="tpu_custom_call" | custom-call | tf_op jit(solution)/shard_map/cond/branch_0_fun/finish_residual/pallas_call | solution.py:467
  (4 shorter events, 0.0 us)
Async XLA Ops:
  0.0 37.7 %copy-start.4 = (s32[16,4]{0,1:T(4,128)S(1)}, s32[16,4]{0,1:T(4,128)}, u32[]{:S(2)}) copy-start(s32[16,4]{0,1:T(4,128)} %param.15) | copy-start | bytes 772
  0.0 37.7 %copy-start.5 = (s32[8,4]{0,1:T(4,128)S(1)}, s32[8,4]{0,1:T(4,128)}, u32[]{:S(2)}) copy-start(s32[8,4]{0,1:T(4,128)} %param.16) | copy-start | bytes 388
  0.0 37.7 %copy-start.1 = (f32[1024,256]{1,0:T(8,128)S(1)}, f32[1024,256]{1,0:T(8,128)}, u32[]{:S(2)}) copy-start(f32[1024,256]{1,0:T(8,128)} %refs_6_.1) | copy-start | bytes 3145732
  0.0 37.7 %copy-start.2 = (f32[512,256]{1,0:T(8,128)S(1)}, f32[512,256]{1,0:T(8,128)}, u32[]{:S(2)}) copy-start(f32[512,256]{1,0:T(8,128)} %refs_7_.1) | copy-start | bytes 1572868
  0.0 37.7 %copy-start.6 = (s32[4]{0:T(128)S(1)}, s32[4]{0:T(128)}, u32[]{:S(2)}) copy-start(s32[4]{0:T(128)} %refs_2_.1) | copy-start | bytes 52
  0.0 37.7 %copy-start.7 = (s32[1,4]{1,0:T(1,128)S(1)}, s32[1,4]{1,0:T(1,128)}, u32[]{:S(2)}) copy-start(s32[1,4]{1,0:T(1,128)} %refs_5_.1) | copy-start | bytes 52
  0.0 37.7 %copy-start.3 = (f32[64,64]{1,0:T(8,128)S(1)}, f32[64,64]{1,0:T(8,128)}, u32[]{:S(2)}) copy-start(f32[64,64]{1,0:T(8,128)} %param.14) | copy-start | bytes 49156
  2.5 17.5 %collective-permute-start = (f32[512,128]{1,0:T(8,128)S(1)}, f32[512,128]{1,0:T(8,128)S(1)}, u32[]{:S(2)}, u32[]{:S(2)}) collective-permute-start(f32[512,128]{1,0:T(8,128)S(1)} %get-tuple-element.79.refs_1_), channel_id=1, source_target_pairs={{0,8},{8,0},{16,24},{24,16},{1,9},{9,1},{17,25},{25,17},{2,10},{10... | collective-permute-start | bytes 786440 | tf_op jit(solution)/shard_map/ppermute | solution.py:437
  2.6 17.4 %collective-permute-start.1 = (f32[512,128]{1,0:T(8,128)S(1)}, f32[512,128]{1,0:T(8,128)S(1)}, u32[]{:S(2)}, u32[]{:S(2)}) collective-permute-start(f32[512,128]{1,0:T(8,128)S(1)} %get-tuple-element.79.refs_1_), channel_id=1, source_target_pairs={{0,16},{8,24},{16,0},{24,8},{1,17},{9,25},{17,1},{25,9},{2,18},{10... | collective-permute-start | bytes 786440 | tf_op jit(solution)/shard_map/ppermute | solution.py:437
  5.5 14.4 %collective-permute-start.2 = (f32[512,128]{1,0:T(8,128)S(1)}, f32[512,128]{1,0:T(8,128)S(1)}, u32[]{:S(2)}, u32[]{:S(2)}) collective-permute-start(f32[512,128]{1,0:T(8,128)S(1)} %get-tuple-element.79.refs_1_), channel_id=1, source_target_pairs={{0,24},{8,16},{16,8},{24,0},{1,25},{9,17},{17,9},{25,1},{2,26},{10... | collective-permute-start | bytes 786440 | tf_op jit(solution)/shard_map/ppermute | solution.py:437
  22.8 14.9 %all-to-all-start.7 = ((f32[8,64,128]{2,1,0:T(8,128)}), f32[8,64,128]{2,1,0:T(8,128)S(1)}, u32[]{:S(2)}, u32[]{:S(2)}) async-start(f32[8,64,128]{2,1,0:T(8,128)} %forward_tiles.3), calls=%async_computation.7 | async-start | bytes 524288 | tf_op jit(solution)/shard_map/all_to_all | solution.py:462
where the time goes:
time: 41.2 us; the launch traced here: 41.4 us
  blocking collectives  14.4 us (35%)
  Pallas kernels  10.1 us (25%)
  starting transfers between devices  9.8 us (24%)
  waiting for transfers between devices  6.44 us (16%)
  between operations  0.69 us (2%)
    all_to_all x1, blocking collectives, local(): lax.all_to_all(mine, ('row', 'col'), split_axis=0, concat_axis=0, tiled=T...  14.4 us
    all_to_all x1, starting transfers between devices, forward(): lax.all_to_all(col_send, 'col', split_axis=0, concat_axis=0, tiled=True)  6.64 us
    all_to_all x1, waiting for transfers between devices, forward(): lax.all_to_all(col_send, 'col', split_axis=0, concat_axis=0, tiled=True)  6.43 us
    pallas_call x1, Pallas kernels, finish(): pl.pallas_call(lambda *refs: finish_kernel(lay, *refs), out_shape=jax.Sha...  3.67 us
    ppermute x3, starting transfers between devices, local(): lax.ppermute(packed, 'row', [(i, i ^ k) for i in range(rows)])  3.16 us
    pallas_call x1, Pallas kernels, forward(): pl.pallas_call(lambda *refs: forward_kernel(lay, slots, *refs), out_shape...  2.8 us
    pallas_call x1, Pallas kernels, local(): pl.pallas_call(lambda *refs: pack_kernel(lay, *refs), out_shape=(jax.Shap...  2.42 us
    pallas_call x1, Pallas kernels, local(): pl.pallas_call(lambda *refs: check_kernel(lay, *refs), out_shape=jax.Shap...  1.17 us
  transfers between devices with their start and end apart: 4, of which 1 were waited for; matrix products, arithmetic and copies ran while one was open for 0% of the time, Pallas kernels for 3%

commit v1 on v0

--- a/solution.py
+++ b/solution.py
@@ -266,9 +266,9 @@
         lax.fori_loop(0, counts[k], send, 0)
 
 
-def finish_kernel(lay, info, extent, fock_scalar, fock, received, *refs):
+def occupied_kernel(lay, info, extent, fock_scalar, fock, *refs):
     packed = refs[: lay.rows]
-    out, amp_id, int_id, next_slot, tiles, ints, sums = refs[lay.rows :]
+    out, todo, amp_id, int_id, next_slot, tiles, sums = refs[lay.rows :]
     row, col = lax.axis_index("row"), lax.axis_index("col")
     local = lay.owner(info, row, col)
     limit = extent[local]
@@ -281,7 +281,9 @@
         first = n_amp
         for tile in range(lay.row_tiles):
             code = lay.amp(info, row ^ k, tile, col, local)
-            amp_id[n_amp] = ((row ^ k) * lay.row_tiles + tile) * 256 + code - 1
+            amp_id[n_amp] = ((row ^ k) * lay.row_tiles + tile) * 256 + jnp.clip(
+                code - 1, 0, ROW_SLOTS - 1
+            )
             n_amp += present(code)
 
         def take_amp(index, carry, k=k):
@@ -289,17 +291,12 @@
             return carry
 
         lax.fori_loop(first, n_amp, take_amp, 0)
-        first = n_int
         for tile in range(lay.integral_tiles):
             code = lay.integral(info, row ^ k, tile, col, local)
-            int_id[n_int] = ((row ^ k) * lay.integral_tiles + tile) * 256 + code - 1
+            int_id[n_int] = (((row ^ k) * lay.integral_tiles + tile) * 256 + k) * 256 + jnp.clip(
+                code - 1, 0, ROW_SLOTS - 1
+            )
             n_int += present(code)
-
-        def take_int(index, carry, k=k):
-            ints[slot_rows(index), :] = packed[k][slot_rows(int_id[index] & 255), :]
-            return carry
-
-        lax.fori_loop(first, n_int, take_int, 0)
 
     blank = jnp.zeros((TS, TS), jnp.float32)
     both = jnp.concatenate(
@@ -324,40 +321,46 @@
 
     lax.fori_loop(0, (n_amp + 3) >> 2, second, 0)
 
-    def ladder(which, carry):
-        middle = int_id[which] >> 8
+    def ladder(which, listed):
+        item = int_id[which]
+        middle = item >> 16
         source, middle_local = middle // lay.groups, middle % lay.groups
         own = (source == col) & (middle_local == local)
-
-        def add(index, packed_tile):
-            product = jnp.dot(
-                unfold(ints[slot_rows(which), :]),
-                unfold(packed_tile),
-                precision=HIGHEST,
-                preferred_element_type=jnp.float32,
-            )
-            product = jnp.where(iota((TS, TS), 0) < limit, product, 0.0)
-            sums[slot_rows(index), :] += fold(product)
-
-        def per_tile(index, carry):
+        own_row = middle // lay.integral_tiles
+
+        for k in range(lay.rows):
+
+            @pl.when(own & (row ^ k == own_row))
+            def _():
+                integral = unfold(packed[k][slot_rows(item & 255), :])
+
+                def diagonal(index, carry):
+                    product = jnp.dot(
+                        integral,
+                        unfold(tiles[slot_rows(index), :]),
+                        precision=HIGHEST,
+                        preferred_element_type=jnp.float32,
+                    )
+                    product = jnp.where(iota((TS, TS), 0) < limit, product, 0.0)
+                    sums[slot_rows(index), :] += fold(product)
+                    return carry
+
+                lax.fori_loop(0, n_amp, diagonal, 0)
+
+        def arriving(index, listed):
             tile = amp_id[index] >> 8
             code = lay.amp(info, tile // lay.row_tiles, tile % lay.row_tiles, source, middle_local)
-
-            @pl.when(own)
-            def _():
-                add(index, tiles[slot_rows(index), :])
-
-            @pl.when((code > 0) & ~own)
-            def _():
-                slot = next_slot[source]
-                next_slot[source] = slot + 1
-                add(index, received[source, slot_rows(slot), :])
-
-            return carry
-
-        return lax.fori_loop(0, n_amp, per_tile, carry)
-
-    lax.fori_loop(0, n_int, ladder, 0)
+            slot = next_slot[source]
+            todo[2 * listed] = (tile * 256 + source) * 256 + jnp.minimum(slot, 255)
+            todo[2 * listed + 1] = item & 65535
+            hit = present(code)
+            next_slot[source] = slot + hit
+            return jnp.minimum(listed + hit, lay.cols * COL_SLOTS[1])
+
+        return lax.fori_loop(0, jnp.where(own, 0, n_amp), arriving, listed)
+
+    todo[2 * lay.cols * COL_SLOTS[1] + 2] = lax.fori_loop(0, n_int, ladder, jnp.int32(0))
+    todo[2 * lay.cols * COL_SLOTS[1] + 3] = limit
 
     def write(index, carry):
         tile = amp_id[index] >> 8
@@ -378,6 +381,35 @@
         return carry
 
     lax.fori_loop(0, n_amp, write, 0)
+
+
+def ladder_kernel(lay, todo, received, partial, *refs):
+    packed, (out, integral) = refs[: lay.rows], refs[lay.rows :]
+    out[...] = partial[...]
+    limit = todo[2 * lay.cols * COL_SLOTS[1] + 3]
+
+    def add(index, carry):
+        item, where = todo[2 * index], todo[2 * index + 1]
+        slot, source, tile = item & 255, (item >> 8) & 255, item >> 16
+        for k in range(lay.rows):
+
+            @pl.when(where >> 8 == k)
+            def _():
+                integral[...] = packed[k][slot_rows(where & 255), :]
+
+        product = jnp.dot(
+            unfold(integral[...]),
+            unfold(received[source, slot_rows(slot), :]),
+            precision=HIGHEST,
+            preferred_element_type=jnp.float32,
+        )
+        product = jnp.where(iota((TS, TS), 0) < limit, product, 0.0)
+        side = iota((TS, LANES), 1) // TS == tile & 1
+        lanes = pl.ds(pl.multiple_of((tile >> 1) * LANES, LANES), LANES)
+        out[0, :, lanes] += jnp.where(side, jnp.concatenate([product, product], axis=1), 0.0)
+        return carry
+
+    lax.fori_loop(0, todo[2 * lay.cols * COL_SLOTS[1] + 2], add, 0)
 
 
 def local(
@@ -463,32 +495,54 @@
 
     received = forward(COL_SLOTS[0], info, *shares)
 
-    def finish(info, received, shares, arguments):
+    out_shape = (1, TS, rows * row_tiles * TS)
+    all_tiles_rows = rows * (row_tiles + 1) * HALF
+    partial, todo = pl.pallas_call(
+        lambda *refs: occupied_kernel(lay, *refs),
+        out_shape=(
+            jax.ShapeDtypeStruct(out_shape, jnp.float32),
+            jax.ShapeDtypeStruct((2 * cols * COL_SLOTS[1] + 4,), jnp.int32),
+        ),
+        in_specs=[in_smem] * 3 + [in_vmem] * (1 + rows),
+        out_specs=(in_vmem, in_smem),
+        scratch_shapes=[
+            smem((rows * row_tiles + 1,)),
+            smem((rows * integral_tiles + 1,)),
+            smem((cols,)),
+            pltpu.VMEM((all_tiles_rows, LANES), jnp.float32),
+            pltpu.VMEM((all_tiles_rows, LANES), jnp.float32),
+        ],
+        compiler_params=params,
+        name="occupied_terms",
+    )(info, tile_extent, hole_fock, hole_fock, *shares)
+
+    def finish(info, received, todo, partial, shares, arguments):
         return pl.pallas_call(
-            lambda *refs: finish_kernel(lay, *refs),
-            out_shape=jax.ShapeDtypeStruct((1, TS, rows * row_tiles * TS), jnp.float32),
-            in_specs=[in_smem] * 3 + [in_vmem] * (2 + rows),
+            lambda *refs: ladder_kernel(lay, *refs),
+            out_shape=jax.ShapeDtypeStruct(out_shape, jnp.float32),
+            in_specs=[in_smem] + [in_vmem] * (2 + rows),
             out_specs=in_vmem,
-            scratch_shapes=[
-                smem((rows * row_tiles + 1,)),
-                smem((rows * integral_tiles + 1,)),
-                smem((cols,)),
-                pltpu.VMEM((rows * (row_tiles + 1) * HALF, LANES), jnp.float32),
-                pltpu.VMEM((rows * integral_tiles * HALF, LANES), jnp.float32),
-                pltpu.VMEM((rows * (row_tiles + 1) * HALF, LANES), jnp.float32),
-            ],
+            scratch_shapes=[pltpu.VMEM((HALF, LANES), jnp.float32)],
             compiler_params=params,
-            name="finish_residual",
-        )(info, arguments[5], arguments[2], arguments[2], received, *shares)
-
-    def more_slots(info, received, shares, arguments):
-        return finish(info, forward(COL_SLOTS[1], info, *shares), shares, arguments)
-
-    def all_tiles(info, received, shares, arguments):
+            name="ladder_terms",
+        )(todo, received, partial, *shares)
+
+    def more_slots(info, received, todo, partial, shares, arguments):
+        received = forward(COL_SLOTS[1], info, *shares)
+        return finish(info, received, todo, partial, shares, arguments)
+
+    def all_tiles(info, received, todo, partial, shares, arguments):
         return dense(*arguments)
 
     return lax.switch(
-        level[0], (finish, more_slots, all_tiles), info, received, tuple(shares), arguments
+        level[0],
+        (finish, more_slots, all_tiles),
+        info,
+        received,
+        todo,
+        partial,
+        tuple(shares),
+        arguments,
     )
 
 

time: 41.2 us -> 38.1 us (0.925); the launches traced: 41.4 us -> 37.4 us
  waiting for transfers between devices: 6.44 us -> 3.25 us
  local copies, waits for them, and re-layouts: 0.03 us -> 0.99 us
  starting transfers between devices: 9.8 us -> 8.96 us
  Pallas kernels: 10.1 us -> 9.3 us
    all_to_all x1, waiting for transfers between devices: 6.43 us -> 3.24 us  [forward(): lax.all_to_all(col_send, 'col', split_axis=0, concat_axis=0, tiled=True)]
    pallas_call x1, Pallas kernels: 2.8 us -> 1.71 us  [forward(): pl.pallas_call(lambda *refs: forward_kernel(lay, slots, *refs), out_shape...]
    all_to_all x1, starting transfers between devices: 6.64 us -> 5.63 us  [forward(): lax.all_to_all(col_send, 'col', split_axis=0, concat_axis=0, tiled=True)]
    unnamed x14, local copies, waits for them, and re-layouts: 0.03 us -> 0.99 us
    pallas_call x1 -> x2, Pallas kernels: 3.67 us -> 3.83 us  [the longest x1 3.22 us: local(): pl.pallas_call(lambda *refs: occupied_kernel(lay, *refs), out_shape=(jax....]
  transfers between devices with their start and end apart: 4 -> 4, of which waited for: 1 -> 1; matrix products, arithmetic and copies ran while one was open for 0% -> 0% of each run, Pallas kernels for 3% -> 12%
where the time goes in v1:
time: 38.1 us; the launch traced here: 37.4 us
  blocking collectives  14 us (37%)
  Pallas kernels  9.3 us (24%)
  starting transfers between devices  8.96 us (24%)
  waiting for transfers between devices  3.25 us (9%)
  local copies, waits for them, and re-layouts  0.99 us (3%)
  between operations  0.69 us (2%)
    all_to_all x1, blocking collectives, local(): lax.all_to_all(mine, ('row', 'col'), split_axis=0, concat_axis=0, tiled=T...  14 us
    all_to_all x1, starting transfers between devices, forward(): lax.all_to_all(col_send, 'col', split_axis=0, concat_axis=0, tiled=True)  5.63 us
    ppermute x3, starting transfers between devices, local(): lax.ppermute(packed, 'row', [(i, i ^ k) for i in range(rows)])  3.33 us
    all_to_all x1, waiting for transfers between devices, forward(): lax.all_to_all(col_send, 'col', split_axis=0, concat_axis=0, tiled=True)  3.24 us
    pallas_call x1, Pallas kernels, local(): pl.pallas_call(lambda *refs: occupied_kernel(lay, *refs), out_shape=(jax....  3.22 us
    pallas_call x1, Pallas kernels, local(): pl.pallas_call(lambda *refs: pack_kernel(lay, *refs), out_shape=(jax.Shap...  2.6 us
    pallas_call x1, Pallas kernels, forward(): pl.pallas_call(lambda *refs: forward_kernel(lay, slots, *refs), out_shape...  1.71 us
    pallas_call x1, Pallas kernels, local(): pl.pallas_call(lambda *refs: check_kernel(lay, *refs), out_shape=jax.Shap...  1.17 us
  transfers between devices with their start and end apart: 4, of which 1 were waited for; matrix products, arithmetic and copies ran while one was open for 0% of the time, Pallas kernels for 12%

profile of v1, /device:TPU:0, one launch (start us, length us, event | category | flops | bytes accessed | tf_op | source)
XLA Modules:
  0.0 37.4 jit_solution(9206191324320505136)
XLA Ops:
  0.0 0.0 copy-start.7
  0.0 2.6 %pack_tiles.1 = (f32[512,128]{1,0:T(8,128)S(1)}, s32[32,1,128]{2,1,0:T(1,128)S(1)}) custom-call(s32[4,16]{1,0:T(4,128)} %bitcast.73, s32[4,8]{1,0:T(4,128)} %bitcast.75, s32[4]{0:T(128)} %refs_1_.1, s32[4,16]{1,0:T(4,128)} %bitcast.74, s32[4,8]{1,0:T(4,128)} %bitcast.76, s32[1,4]{1,0:T(1,128)} %refs_5_.1, f32[1024,256]{1,0:T(8,128)} %refs_6_.1, ...), custom_call_target="tpu_custom_call" | custom-call | tf_op jit(solution)/shard_map/pack_tiles/pallas_call | solution.py:443
  2.6 0.7 %collective-permute-start = (f32[512,128]{1,0:T(8,128)S(1)}, f32[512,128]{1,0:T(8,128)S(1)}, u32[]{:S(2)}, u32[]{:S(2)}) collective-permute-start(f32[512,128]{1,0:T(8,128)S(1)} %get-tuple-element.78.refs_4_.refs_1_), channel_id=1, source_target_pairs={{0,8},{8,0},{16,24},{24,16},{1,9},{9,1},{17,25},{25,17},{2,10},{10... | collective-permute-start | bytes 786440 | tf_op jit(solution)/shard_map/ppermute | solution.py:469
  3.3 2.6 %collective-permute-start.1 = (f32[512,128]{1,0:T(8,128)S(1)}, f32[512,128]{1,0:T(8,128)S(1)}, u32[]{:S(2)}, u32[]{:S(2)}) collective-permute-start(f32[512,128]{1,0:T(8,128)S(1)} %get-tuple-element.78.refs_4_.refs_1_), channel_id=1, source_target_pairs={{0,16},{8,24},{16,0},{24,8},{1,17},{9,25},{17,1},{25,9},{2,18},{10... | collective-permute-start | bytes 786440 | tf_op jit(solution)/shard_map/ppermute | solution.py:469
  5.9 0.1 collective-permute-start.2
  6.0 14.0 %all_to_all.62.refs_0_ = s32[32,1,128]{2,1,0:T(1,128)S(1)} all-to-all(s32[32,1,128]{2,1,0:T(1,128)S(1)} %get-tuple-element.77), channel_id=1, replica_groups=mesh['row'=4,'col'=8] {'row','col'}, dimensions={0} | all-to-all | bytes 32768 | tf_op jit(solution)/shard_map/all_to_all | solution.py:470
  19.9 0.0 collective-permute-done.refs_5_.refs_2_
  19.9 0.0 collective-permute-done.1.refs_6_.refs_3_
  19.9 0.0 collective-permute-done.2.refs_7_.refs_4_
  19.9 1.7 %forward_tiles.3 = f32[8,64,128]{2,1,0:T(8,128)} custom-call(s32[32,1,128]{2,1,0:T(1,128)S(1)} %all_to_all.62.refs_0_, f32[512,128]{1,0:T(8,128)S(1)} %get-tuple-element.78.refs_4_.refs_1_, f32[512,128]{1,0:T(8,128)S(1)} %collective-permute-done.refs_5_.refs_2_, f32[512,128]{1,0:T(8,128)S(1)} %collective-permute-done.1.refs_6_.refs_3_, ...), custom_call_target="tpu_custom_call" | custom-call | tf_op jit(solution)/shard_map/forward_tiles/pallas_call | solution.py:482
  21.6 5.6 %all-to-all-start.7 = ((f32[8,64,128]{2,1,0:T(8,128)}), f32[8,64,128]{2,1,0:T(8,128)S(1)}, u32[]{:S(2)}, u32[]{:S(2)}) async-start(f32[8,64,128]{2,1,0:T(8,128)} %forward_tiles.3), calls=%async_computation.7 | async-start | bytes 524288 | tf_op jit(solution)/shard_map/all_to_all | solution.py:494
  27.3 1.2 %check_slots.1 = s32[1]{0:T(128)} custom-call(s32[32,1,128]{2,1,0:T(1,128)S(1)} %all_to_all.62.refs_0_), custom_call_target="tpu_custom_call" | custom-call | tf_op jit(solution)/shard_map/check_slots/pallas_call | solution.py:472
  29.1 0.0 copy-done.6
  29.1 0.0 copy-done.3
  29.1 3.2 %occupied_terms.1 = (f32[1,64,4096]{2,1,0:T(8,128)S(1)}, s32[68]{0:T(128)S(1)}) custom-call(s32[32,1,128]{2,1,0:T(1,128)S(1)} %all_to_all.62.refs_0_, s32[4]{0:T(128)S(1)} %copy-done.6, f32[64,64]{1,0:T(8,128)S(1)} %copy-done.3, f32[64,64]{1,0:T(8,128)S(1)} %copy-done.3, f32[512,128]{1,0:T(8,128)S(1)} %get-tuple-element.78.refs_4_.refs_1_, ...), custom_call_target="tpu_custom_call" | custom-call | tf_op jit(solution)/shard_map/occupied_terms/pallas_call | solution.py:500
  32.3 3.2 %all-to-all-done.7 = f32[8,64,128]{2,1,0:T(8,128)S(1)} async-done(((f32[8,64,128]{2,1,0:T(8,128)}), f32[8,64,128]{2,1,0:T(8,128)S(1)}, u32[]{:S(2)}, u32[]{:S(2)}) %all-to-all-start.7) | async-done | bytes 262176 | tf_op jit(solution)/shard_map/all_to_all | solution.py:494
  35.5 0.0 copy-done.1
  35.5 0.0 copy-done.4
  35.5 0.0 copy-done.5
  35.6 0.0 copy-done.7
  35.6 0.9 %conditional.1 = (f32[1,64,4096]{2,1,0:T(8,128)S(1)}) conditional(s32[]{:T(128)} %bitcast.29, (s32[68]{0:T(128)S(1)}, f32[8,64,128]{2,1,0:T(8,128)S(1)}, f32[1,64,4096]{2,1,0:T(8,128)S(1)}, f32[512,128]{1,0:T(8,128)S(1)}, f32[512,128]{1,0:T(8,128)S(1)}, /*index=5*/f32[512,128]{1,0:T(8,128)S(1)}, f32[512,128]{1,0:T(8,128)S(1)}) %tuple.15, ...), branch_computations={%region_0.0_spmd, %region_1.0_spmd, %region_2.4_spmd} | conditional | flops 6847334912 | bytes 147542720 | solution.py:537
  35.6 0.6 %ladder_terms.2 = f32[1,64,4096]{2,1,0:T(8,128)S(1)} custom-call(s32[68]{0:T(128)S(1)} %get-tuple-element.50.refs_0_, f32[8,64,128]{2,1,0:T(8,128)S(1)} %get-tuple-element.52.refs_1_, f32[1,64,4096]{2,1,0:T(8,128)S(1)} %get-tuple-element.54.refs_2_, f32[512,128]{1,0:T(8,128)S(1)} %get-tuple-element.55.refs_3_, f32[512,128]{1,0:T(8,128)S(1)} %get-tuple-element.56.refs_4_, ...), custom_call_target="tpu_custom_call" | custom-call | tf_op jit(solution)/shard_map/cond/branch_0_fun/ladder_terms/pallas_call | solution.py:520
  36.4 0.0 copy-start.2
  36.4 1.0 %copy-done.2 = f32[1,64,4096]{2,1,0:T(8,128)} copy-done((f32[1,64,4096]{2,1,0:T(8,128)}, f32[1,64,4096]{2,1,0:T(8,128)S(1)}, u32[]{:S(2)}) %copy-start.2) | copy-done | bytes 1048600
  (5 shorter events, 0.0 us)
Async XLA Ops:
  0.0 29.1 %copy-start.6 = (s32[4]{0:T(128)S(1)}, s32[4]{0:T(128)}, u32[]{:S(2)}) copy-start(s32[4]{0:T(128)} %refs_1_.1) | copy-start | bytes 52
  0.0 29.1 %copy-start.3 = (f32[64,64]{1,0:T(8,128)S(1)}, f32[64,64]{1,0:T(8,128)}, u32[]{:S(2)}) copy-start(f32[64,64]{1,0:T(8,128)} %refs_3_.1) | copy-start | bytes 49156
  0.0 35.5 %copy-start.1 = (f32[1024,256]{1,0:T(8,128)S(1)}, f32[1024,256]{1,0:T(8,128)}, u32[]{:S(2)}) copy-start(f32[1024,256]{1,0:T(8,128)} %refs_6_.1) | copy-start | bytes 3145732
  0.0 35.5 %copy-start.4 = (s32[16,4]{0,1:T(4,128)S(1)}, s32[16,4]{0,1:T(4,128)}, u32[]{:S(2)}) copy-start(s32[16,4]{0,1:T(4,128)} %param.15) | copy-start | bytes 772
  0.0 35.5 %copy-start.5 = (s32[8,4]{0,1:T(4,128)S(1)}, s32[8,4]{0,1:T(4,128)}, u32[]{:S(2)}) copy-start(s32[8,4]{0,1:T(4,128)} %param.16) | copy-start | bytes 388
  0.0 35.5 %copy-start.7 = (s32[1,4]{1,0:T(1,128)S(1)}, s32[1,4]{1,0:T(1,128)}, u32[]{:S(2)}) copy-start(s32[1,4]{1,0:T(1,128)} %refs_5_.1) | copy-start | bytes 52
  2.6 17.3 %collective-permute-start = (f32[512,128]{1,0:T(8,128)S(1)}, f32[512,128]{1,0:T(8,128)S(1)}, u32[]{:S(2)}, u32[]{:S(2)}) collective-permute-start(f32[512,128]{1,0:T(8,128)S(1)} %get-tuple-element.78.refs_4_.refs_1_), channel_id=1, source_target_pairs={{0,8},{8,0},{16,24},{24,16},{1,9},{9,1},{17,25},{25,17},{2,10},{10... | collective-permute-start | bytes 786440 | tf_op jit(solution)/shard_map/ppermute | solution.py:469
  3.3 16.6 %collective-permute-start.1 = (f32[512,128]{1,0:T(8,128)S(1)}, f32[512,128]{1,0:T(8,128)S(1)}, u32[]{:S(2)}, u32[]{:S(2)}) collective-permute-start(f32[512,128]{1,0:T(8,128)S(1)} %get-tuple-element.78.refs_4_.refs_1_), channel_id=1, source_target_pairs={{0,16},{8,24},{16,0},{24,8},{1,17},{9,25},{17,1},{25,9},{2,18},{10... | collective-permute-start | bytes 786440 | tf_op jit(solution)/shard_map/ppermute | solution.py:469
  5.9 14.0 %collective-permute-start.2 = (f32[512,128]{1,0:T(8,128)S(1)}, f32[512,128]{1,0:T(8,128)S(1)}, u32[]{:S(2)}, u32[]{:S(2)}) collective-permute-start(f32[512,128]{1,0:T(8,128)S(1)} %get-tuple-element.78.refs_4_.refs_1_), channel_id=1, source_target_pairs={{0,24},{8,16},{16,8},{24,0},{1,25},{9,17},{17,9},{25,1},{2,26},{10... | collective-permute-start | bytes 786440 | tf_op jit(solution)/shard_map/ppermute | solution.py:469
  21.6 13.9 %all-to-all-start.7 = ((f32[8,64,128]{2,1,0:T(8,128)}), f32[8,64,128]{2,1,0:T(8,128)S(1)}, u32[]{:S(2)}, u32[]{:S(2)}) async-start(f32[8,64,128]{2,1,0:T(8,128)} %forward_tiles.3), calls=%async_computation.7 | async-start | bytes 524288 | tf_op jit(solution)/shard_map/all_to_all | solution.py:494
  36.4 1.0 %copy-start.2 = (f32[1,64,4096]{2,1,0:T(8,128)}, f32[1,64,4096]{2,1,0:T(8,128)S(1)}, u32[]{:S(2)}) copy-start(f32[1,64,4096]{2,1,0:T(8,128)S(1)} %get-tuple-element.138) | copy-start | bytes 3145732
